TPU v7x, 32 devices: a whole 2x2x4 slice. The times are simulated.
32 devices in a mesh: dp: 8 (over z, y), seq: 4 (over x, core).
Axes of the slice: x: 2, y: 2, z: 4, core: 2. Of those that a mesh axis runs over, the one named last changes fastest.
Arguments:
- tokens_in: bfloat16 [16, 2048, 640], P('dp', 'seq'), may hold values from -6 to 6
- segment_ids: int32 [16, 2048], P('dp', 'seq'), may hold values from 0 to 4, as said below
- query_weight: bfloat16 [640, 1024], P('dp', 'seq'), may hold values from -0.25 to 0.25
- key_weight: bfloat16 [640, 256], P('dp', 'seq'), may hold values from -0.25 to 0.25
- value_weight: bfloat16 [640, 256], P('dp', 'seq'), may hold values from -0.25 to 0.25
- out_weight: bfloat16 [1024, 640], P('dp', 'seq'), may hold values from -0.1875 to 0.1875
- gate_weight: bfloat16 [640, 2048], P('dp', 'seq'), may hold values from -0.25 to 0.25
- up_weight: bfloat16 [640, 2048], P('dp', 'seq'), may hold values from -0.25 to 0.25
- down_weight: bfloat16 [2048, 640], P('dp', 'seq'), may hold values from -0.125 to 0.125
- norm_gains: bfloat16 [3072], P(('dp', 'seq')), may hold values from 0.5 to 1.5
- d_output: bfloat16 [16, 2048, 640], P('dp', 'seq'), may hold values from -6 to 6
Outputs:
- output: bfloat16 [16, 2048, 640], P('dp', 'seq')
- grad_input: float32 [16, 2048, 640], P('dp', 'seq')
- grad_query: float32 [640, 1024], P('dp', 'seq')
- grad_key: float32 [640, 256], P('dp', 'seq')
- grad_value: float32 [640, 256], P('dp', 'seq')
- grad_out: float32 [1024, 640], P('dp', 'seq')
- grad_gate: float32 [640, 2048], P('dp', 'seq')
- grad_up: float32 [640, 2048], P('dp', 'seq')
- grad_down: float32 [2048, 640], P('dp', 'seq')
- grad_gains: float32 [3072], P(('dp', 'seq'))
Inputs may be any that keep to these rules, and one draw needn't show every extreme that they name: `segment_ids`: along each sequence the ids start at 0 and rise by one at each document boundary. Each block of 512 tokens starting at a multiple of 512 holds at most one boundary, at least 128 tokens from both of its ends.
All inputs are finite; a program needn't handle non-finite values.
Results may differ from a plain program's by a relative error of at most 0.017.
Values may be sent and summed in bfloat16 or wider, within the bound.
A program may use at most 192 MiB of HBM per device.

v0:
```python
from functools import partial
import math

import jax
import jax.numpy as jnp
from jax import lax
from jax.sharding import PartitionSpec as P

D = 640
NQ = 4
HD = 256
FF = 2048
WINDOW = 512
MICRO = 2


EPSILON = 1e-06
MASKED = -1e30


def shifted(block, axis, distance):
    devices = range(lax.axis_size(axis))
    route = [(i - distance, i) for i in devices if i - distance in devices]
    return lax.ppermute(block, axis, route)


def rms_scale(values, scales):
    mean_square = jnp.mean(values * values, axis=-1, keepdims=True)
    return values * lax.rsqrt(mean_square + EPSILON) * scales


def rotate(values, cosine, sine_table):
    middle = values.shape[-1] // 2
    turned = jnp.concatenate([-values[..., middle:], values[..., :middle]], axis=-1)
    return values * cosine + turned * sine_table


def query_map(raw_part, scales, cosine, sine_table):
    return rotate(rms_scale(raw_part, scales), cosine, sine_table) * (
        1.0 / math.sqrt(raw_part.shape[-1])
    )


def key_map(raw_part, scales, cosine, sine_table):
    return rotate(rms_scale(raw_part, scales), cosine, sine_table)


def gated_inner(gate_part, up_part):
    return jax.nn.gelu(gate_part, approximate=True) * up_part


def rotary_tables(positions, head_width):
    frequency = jnp.exp(
        jnp.arange(head_width // 2, dtype=jnp.float32) * (-2.0 * math.log(10000.0) / head_width)
    )
    angles = positions.astype(jnp.float32)[:, None] * frequency[None, :]
    angles = jnp.concatenate([angles, angles], axis=-1)
    return (jnp.cos(angles), jnp.sin(angles))


def rows_product(left_side, right_side):
    return lax.dot_general(
        left_side, right_side, (((0,), (0,)), ((), ())), preferred_element_type=jnp.float32
    )


def times_transposed(left_side, right_side):
    return lax.dot_general(
        left_side, right_side, (((1,), (1,)), ((), ())), preferred_element_type=jnp.float32
    )


def plain_product(left_side, right_side):
    return jnp.dot(left_side, right_side, preferred_element_type=jnp.float32)


def local(
    tokens_in,
    segment_ids,
    query_weight,
    key_weight,
    value_weight,
    out_weight,
    gate_weight,
    up_weight,
    down_weight,
    norm_gains,
    d_output,
):
    seqs_here = tokens_in.shape[0]
    block_len = tokens_in.shape[1]
    per_batch = seqs_here // MICRO
    token_count = per_batch * block_len
    seq_place = lax.axis_index("seq")
    positions = seq_place * block_len + jnp.arange(block_len, dtype=jnp.int32)
    cosine, sine_table = rotary_tables(positions, HD)
    prior_ids = shifted(segment_ids, "seq", 1)
    key_ids = jnp.concatenate([prior_ids, segment_ids], axis=1)
    row_index = jnp.arange(block_len, dtype=jnp.int32)[:, None]
    col_index = jnp.arange(2 * block_len, dtype=jnp.int32)[None, :]
    distance = row_index + block_len - col_index
    reach = (distance >= 0) & (distance < WINDOW) & ((col_index >= block_len) | (seq_place > 0))
    allowed_all = reach[None] & (segment_ids[:, :, None] == key_ids[:, None, :])

    def fetch_weights():
        halfway = (
            lax.all_gather(query_weight, "seq", axis=1, tiled=True),
            lax.all_gather(key_weight, "seq", axis=1, tiled=True),
            lax.all_gather(value_weight, "seq", axis=1, tiled=True),
            lax.all_gather(out_weight, "seq", axis=1, tiled=True),
            lax.all_gather(gate_weight, "seq", axis=1, tiled=True),
            lax.all_gather(up_weight, "seq", axis=1, tiled=True),
            lax.all_gather(down_weight, "seq", axis=1, tiled=True),
            lax.all_gather(norm_gains, "seq", axis=0, tiled=True),
        )
        return (
            lax.all_gather(halfway[0], "dp", axis=0, tiled=True),
            lax.all_gather(halfway[1], "dp", axis=0, tiled=True),
            lax.all_gather(halfway[2], "dp", axis=0, tiled=True),
            lax.all_gather(halfway[3], "dp", axis=0, tiled=True),
            lax.all_gather(halfway[4], "dp", axis=0, tiled=True),
            lax.all_gather(halfway[5], "dp", axis=0, tiled=True),
            lax.all_gather(halfway[6], "dp", axis=0, tiled=True),
            lax.all_gather(halfway[7], "dp", axis=0, tiled=True),
        )

    grad_query = jnp.zeros((D, NQ * HD), jnp.float32)
    grad_key = jnp.zeros((D, HD), jnp.float32)
    grad_value = jnp.zeros((D, HD), jnp.float32)
    grad_out = jnp.zeros((NQ * HD, D), jnp.float32)
    grad_gate = jnp.zeros((D, FF), jnp.float32)
    grad_up = jnp.zeros((D, FF), jnp.float32)
    grad_down = jnp.zeros((FF, D), jnp.float32)
    grad_gains = jnp.zeros((4 * D + 2 * HD,), jnp.float32)
    out_blocks = []
    grad_blocks = []
    for micro_index in range(MICRO):
        row_lower = micro_index * per_batch
        row_upper = row_lower + per_batch
        weights_now = fetch_weights()
        gains_float = weights_now[7].astype(jnp.float32)
        in_scale = gains_float[0:D]
        attn_scale = gains_float[D : 2 * D]
        pre_scale = gains_float[2 * D : 3 * D]
        post_scale = gains_float[3 * D : 4 * D]
        query_scale = gains_float[4 * D : 4 * D + HD]
        key_scale = gains_float[4 * D + HD : 4 * D + 2 * HD]
        tokens_now = tokens_in[row_lower:row_upper].astype(jnp.float32).reshape(token_count, D)
        normed_vals, input_pull = jax.vjp(rms_scale, tokens_now, in_scale)
        normed = normed_vals.astype(jnp.bfloat16)
        query_raw = plain_product(normed, weights_now[0]).reshape(per_batch, block_len, NQ, HD)
        key_raw = plain_product(normed, weights_now[1]).reshape(per_batch, block_len, HD)
        values_own = (
            plain_product(normed, weights_now[2])
            .astype(jnp.bfloat16)
            .reshape(per_batch, block_len, HD)
        )
        query_vals, query_pull = jax.vjp(
            partial(query_map, cosine=cosine[:, None, :], sine_table=sine_table[:, None, :]),
            query_raw,
            query_scale,
        )
        key_vals, key_pull = jax.vjp(
            partial(key_map, cosine=cosine, sine_table=sine_table), key_raw, key_scale
        )
        queries = query_vals.astype(jnp.bfloat16)
        keys_own = key_vals.astype(jnp.bfloat16)
        prior_pair = shifted(jnp.concatenate([keys_own, values_own], axis=-1), "seq", 1)
        keys_all = jnp.concatenate([prior_pair[..., :HD], keys_own], axis=1)
        values_all = jnp.concatenate([prior_pair[..., HD:], values_own], axis=1)
        allowed = allowed_all[row_lower:row_upper][:, None]
        scores = jnp.einsum("sqhd,skd->shqk", queries, keys_all, preferred_element_type=jnp.float32)
        scores = jnp.where(allowed, scores, MASKED)
        row_top = jnp.max(scores, axis=-1, keepdims=True)
        weights_exp = jnp.exp(scores - row_top)
        row_total = jnp.sum(weights_exp, axis=-1, keepdims=True)
        prob_weights = (weights_exp / row_total).astype(jnp.bfloat16)
        mixed_heads = jnp.einsum(
            "shqk,skd->sqhd", prob_weights, values_all, preferred_element_type=jnp.float32
        )
        mixed_heads = mixed_heads.astype(jnp.bfloat16).reshape(token_count, NQ * HD)
        branch = plain_product(mixed_heads, weights_now[3])
        post_vals, post_pull = jax.vjp(rms_scale, branch, attn_scale)
        residual = tokens_now + post_vals
        inner_vals, inner_pull = jax.vjp(rms_scale, residual, pre_scale)
        inner_normed = inner_vals.astype(jnp.bfloat16)
        gate_vals = plain_product(inner_normed, weights_now[4])
        up_vals = plain_product(inner_normed, weights_now[5])
        hidden_vals, hidden_pull = jax.vjp(gated_inner, gate_vals, up_vals)
        hidden = hidden_vals.astype(jnp.bfloat16)
        ffn_vals = plain_product(hidden, weights_now[6])
        final_vals, final_pull = jax.vjp(rms_scale, ffn_vals, post_scale)
        out_blocks.append(
            (residual + final_vals).astype(jnp.bfloat16).reshape(per_batch, block_len, D)
        )
        weights_back = fetch_weights()
        cotangent = d_output[row_lower:row_upper].astype(jnp.float32).reshape(token_count, D)
        d_ffn, d_post_scale = final_pull(cotangent)
        d_ffn = d_ffn.astype(jnp.bfloat16)
        grad_down = grad_down + rows_product(hidden, d_ffn)
        d_hidden = times_transposed(d_ffn, weights_back[6])
        d_gate, d_up = hidden_pull(d_hidden)
        d_gate = d_gate.astype(jnp.bfloat16)
        d_up = d_up.astype(jnp.bfloat16)
        grad_gate = grad_gate + rows_product(inner_normed, d_gate)
        grad_up = grad_up + rows_product(inner_normed, d_up)
        d_inner = times_transposed(d_gate, weights_back[4]) + times_transposed(
            d_up, weights_back[5]
        )
        d_resid_part, d_pre_scale = inner_pull(d_inner)
        d_resid = cotangent + d_resid_part
        d_branch, d_attn_scale = post_pull(d_resid)
        d_branch = d_branch.astype(jnp.bfloat16)
        grad_out = grad_out + rows_product(mixed_heads, d_branch)
        d_mixed = (
            times_transposed(d_branch, weights_back[3])
            .astype(jnp.bfloat16)
            .reshape(per_batch, block_len, NQ, HD)
        )
        scores_again = jnp.einsum(
            "sqhd,skd->shqk", queries, keys_all, preferred_element_type=jnp.float32
        )
        scores_again = jnp.where(allowed, scores_again, MASKED)
        probs_float = jnp.exp(scores_again - row_top) / row_total
        probs_again = probs_float.astype(jnp.bfloat16)
        d_probs = jnp.einsum(
            "sqhd,skd->shqk", d_mixed, values_all, preferred_element_type=jnp.float32
        )
        row_inner = jnp.sum(probs_float * d_probs, axis=-1, keepdims=True)
        d_scores = (probs_float * (d_probs - row_inner)).astype(jnp.bfloat16)
        d_queries = jnp.einsum(
            "shqk,skd->sqhd", d_scores, keys_all, preferred_element_type=jnp.float32
        )
        d_keys = jnp.einsum("shqk,sqhd->skd", d_scores, queries, preferred_element_type=jnp.float32)
        d_values = jnp.einsum(
            "shqk,sqhd->skd", probs_again, d_mixed, preferred_element_type=jnp.float32
        )
        earlier_part = jnp.concatenate([d_keys[:, :block_len], d_values[:, :block_len]], axis=-1)
        later_pair = shifted(earlier_part, "seq", -1)
        d_keys_own = d_keys[:, block_len:] + later_pair[..., :HD]
        d_values_own = (
            (d_values[:, block_len:] + later_pair[..., HD:])
            .astype(jnp.bfloat16)
            .reshape(token_count, HD)
        )
        d_query_raw, d_query_scale = query_pull(d_queries)
        d_query_raw = d_query_raw.astype(jnp.bfloat16).reshape(token_count, NQ * HD)
        d_key_raw, d_key_scale = key_pull(d_keys_own)
        d_key_raw = d_key_raw.astype(jnp.bfloat16).reshape(token_count, HD)
        grad_query = grad_query + rows_product(normed, d_query_raw)
        grad_key = grad_key + rows_product(normed, d_key_raw)
        grad_value = grad_value + rows_product(normed, d_values_own)
        d_normed = (
            times_transposed(d_query_raw, weights_back[0])
            + times_transposed(d_key_raw, weights_back[1])
            + times_transposed(d_values_own, weights_back[2])
        )
        d_tokens, d_in_scale = input_pull(d_normed)
        grad_blocks.append((d_resid + d_tokens).reshape(per_batch, block_len, D))
        grad_gains = grad_gains + jnp.concatenate(
            [d_in_scale, d_attn_scale, d_pre_scale, d_post_scale, d_query_scale, d_key_scale]
        )
    output = jnp.concatenate(out_blocks, axis=0)
    grad_input = jnp.concatenate(grad_blocks, axis=0)
    reduced_dp = (
        lax.psum_scatter(grad_query, "dp", scatter_dimension=0, tiled=True),
        lax.psum_scatter(grad_key, "dp", scatter_dimension=0, tiled=True),
        lax.psum_scatter(grad_value, "dp", scatter_dimension=0, tiled=True),
        lax.psum_scatter(grad_out, "dp", scatter_dimension=0, tiled=True),
        lax.psum_scatter(grad_gate, "dp", scatter_dimension=0, tiled=True),
        lax.psum_scatter(grad_up, "dp", scatter_dimension=0, tiled=True),
        lax.psum_scatter(grad_down, "dp", scatter_dimension=0, tiled=True),
        lax.psum_scatter(grad_gains, "dp", scatter_dimension=0, tiled=True),
    )
    reduced = (
        lax.psum_scatter(reduced_dp[0], "seq", scatter_dimension=1, tiled=True),
        lax.psum_scatter(reduced_dp[1], "seq", scatter_dimension=1, tiled=True),
        lax.psum_scatter(reduced_dp[2], "seq", scatter_dimension=1, tiled=True),
        lax.psum_scatter(reduced_dp[3], "seq", scatter_dimension=1, tiled=True),
        lax.psum_scatter(reduced_dp[4], "seq", scatter_dimension=1, tiled=True),
        lax.psum_scatter(reduced_dp[5], "seq", scatter_dimension=1, tiled=True),
        lax.psum_scatter(reduced_dp[6], "seq", scatter_dimension=1, tiled=True),
        lax.psum_scatter(reduced_dp[7], "seq", scatter_dimension=0, tiled=True),
    )
    gains_done = reduced[7]
    return (
        output,
        grad_input,
        reduced[0],
        reduced[1],
        reduced[2],
        reduced[3],
        reduced[4],
        reduced[5],
        reduced[6],
        gains_done,
    )


def solution(mesh):
    return jax.shard_map(
        local,
        mesh=mesh,
        in_specs=(
            P("dp", "seq", None),
            P("dp", "seq"),
            P("dp", "seq"),
            P("dp", "seq"),
            P("dp", "seq"),
            P("dp", "seq"),
            P("dp", "seq"),
            P("dp", "seq"),
            P("dp", "seq"),
            P(("dp", "seq")),
            P("dp", "seq", None),
        ),
        out_specs=(
            P("dp", "seq", None),
            P("dp", "seq", None),
            P("dp", "seq"),
            P("dp", "seq"),
            P("dp", "seq"),
            P("dp", "seq"),
            P("dp", "seq"),
            P("dp", "seq"),
            P("dp", "seq"),
            P(("dp", "seq")),
        ),
        check_vma=False,
    )
```

profile of v0, /device:TPU:0, one launch (start us, length us, event | category | flops | bytes accessed | tf_op | source)
XLA Modules:
  0.0 1161.9 jit_solution(10456775823842327066)
XLA Ops:
  7.3 8.6 all_gather.38
  16.0 6.3 all_gather.40
  22.3 8.1 all_gather.42
  30.5 7.3 all_gather.44
  39.4 7.0 all-reduce.8
  46.4 26.7 %all-gather = bf16[8,1,384]{2,1,0:T(2,128)(2,1)S(1)} all-gather(bf16[1,1,384]{2,1,0:T(2,128)(2,1)S(1)} %reshape.999), channel_id=1, replica_groups=mesh['dp'=8,'seq'=4] {'dp'}, dimensions={0}, use_global_device_ids=true | all-gather | bytes 6912 | tf_op jit(solution)/shard_map/all_gather | solution.py:124
  73.1 5.2 all_gather.34
  78.4 5.2 all_gather.36
  83.8 31.4 %all_gather.35 = bf16[640,256]{1,0:T(8,128)(2,1)S(1)} all-gather(bf16[80,256]{1,0:T(8,128)(2,1)S(1)} %copy.150), channel_id=1, replica_groups=mesh['dp'=8,'seq'=4] {'dp'}, dimensions={0}, use_global_device_ids=true | all-gather | bytes 368640 | tf_op jit(solution)/shard_map/all_gather | solution.py:118
  115.2 31.8 %all_gather.37 = bf16[640,256]{1,0:T(8,128)(2,1)S(1)} all-gather(bf16[80,256]{1,0:T(8,128)(2,1)S(1)} %copy.151), channel_id=1, replica_groups=mesh['dp'=8,'seq'=4] {'dp'}, dimensions={0}, use_global_device_ids=true | all-gather | bytes 368640 | tf_op jit(solution)/shard_map/all_gather | solution.py:119
  150.9 3.3 broadcast_multiply_fusion.1
  157.1 2.7 collective-permute-start.1
  161.3 2.7 collective-permute-start
  164.0 6.4 all_gather.46
  188.1 2.9 multiply_reduce_fusion.5
  193.0 4.4 fusion.198
  197.4 3.2 reshape.968
  200.6 2.9 multiply_reduce_fusion.4
  203.5 2.9 copy.164
  206.4 2.9 copy.215
  209.3 2.9 copy.213
  215.0 2.5 multiply_multiply_fusion.7
  222.6 2.9 copy.211
  229.3 3.5 copy.210
  232.8 6.6 multiply_convert_fusion.7
  244.5 2.7 fusion.69
  248.9 3.3 copy-done.9
  256.4 6.6 fusion.66
  266.6 6.0 fusion.223
  272.6 6.7 multiply_convert_fusion.2
  279.3 4.4 multiply_reduce_fusion.14
  293.7 4.5 multiply_convert_fusion.1
  303.3 4.7 multiply_convert_fusion
  311.8 2.7 multiply_reduce_fusion.8
  323.3 7.9 fusion
  331.2 7.0 fusion.75
  339.7 7.0 fusion.3
  346.7 7.0 fusion.72
  353.8 4.8 fusion.27
  363.7 4.8 fusion.26
  382.9 3.7 fusion.145
  394.4 3.6 fusion.148
  406.7 2.6 convolution_add_fusion.4
  410.8 3.1 fusion.231
  414.0 4.2 convolution_add_fusion
  419.3 3.3 fusion.230
  422.6 4.0 convolution_add_fusion.1
  427.0 3.3 fusion.229
  430.3 4.0 convolution_add_fusion.2
  434.4 23.4 %reduce-scatter.29.cloned.1.call-done = f32[80,256]{1,0:T(8,128)} async-done(((f32[640,256]{1,0:T(8,128)}), f32[80,256]{1,0:T(8,128)}) %reduce-scatter.29.cloned.1.call-update) | async-done | bytes 81936 | tf_op jit(solution)/shard_map/reduce_scatter | solution.py:268
  459.5 63.6 %reduce-scatter.27.cloned.1.call-done = f32[80,256]{1,0:T(8,128)} async-done(((f32[640,256]{1,0:T(8,128)}), f32[80,256]{1,0:T(8,128)}) %reduce-scatter.27.cloned.1.call-update) | async-done | bytes 81936 | tf_op jit(solution)/shard_map/reduce_scatter | solution.py:267
  524.9 71.3 %reduce-scatter.31.cloned.1.call-done = f32[128,640]{1,0:T(8,128)} async-done(((f32[1024,640]{1,0:T(8,128)}), f32[128,640]{1,0:T(8,128)}) %reduce-scatter.31.cloned.1.call-update) | async-done | bytes 327696 | tf_op jit(solution)/shard_map/reduce_scatter | solution.py:269
  598.1 71.6 %reduce-scatter.23.cloned.1.call-done = f32[80,1024]{1,0:T(8,128)} async-done(((f32[640,1024]{1,0:T(8,128)}), f32[80,1024]{1,0:T(8,128)}) %reduce-scatter.23.cloned.1.call-update) | async-done | bytes 327696 | tf_op jit(solution)/shard_map/reduce_scatter | solution.py:266
  671.7 102.9 %reduce-scatter.41.cloned.1.call-done = f32[256,640]{1,0:T(8,128)} async-done(((f32[2048,640]{1,0:T(8,128)}), f32[256,640]{1,0:T(8,128)}) %reduce-scatter.41.cloned.1.call-update) | async-done | bytes 655376 | tf_op jit(solution)/shard_map/reduce_scatter | solution.py:272
  783.4 97.2 %reduce-scatter.37.cloned.1.call-done = f32[80,2048]{1,0:T(8,128)} async-done(((f32[640,2048]{1,0:T(8,128)}), f32[80,2048]{1,0:T(8,128)}) %reduce-scatter.37.cloned.1.call-update) | async-done | bytes 655376 | tf_op jit(solution)/shard_map/reduce_scatter | solution.py:271
  884.1 102.5 %reduce-scatter.33.cloned.1.call-done = f32[80,2048]{1,0:T(8,128)} async-done(((f32[640,2048]{1,0:T(8,128)}), f32[80,2048]{1,0:T(8,128)}) %reduce-scatter.33.cloned.1.call-update) | async-done | bytes 655376 | tf_op jit(solution)/shard_map/reduce_scatter | solution.py:270
  986.7 35.9 %all-reduce.9 = f32[3072]{0:T(1024)S(1)} all-reduce(f32[3072]{0:T(1024)S(1)} %add.364), channel_id=16, replica_groups=mesh['dp'=8,'seq'=4] {'dp'}, use_global_device_ids=true, to_apply=%region_56.57.clone | all-reduce | flops 3072 | bytes 24576
  1022.7 5.6 all-reduce.10
  1029.0 2.8 fusion.95
  1033.4 21.6 %reduce-scatter.47.cloned.1.call-done = f32[160,128]{1,0:T(8,128)} async-done(((f32[640,128]{1,0:T(8,128)}), f32[160,128]{1,0:T(8,128)}) %reduce-scatter.47.cloned.1.call-update) | async-done | bytes 81936
  1055.0 23.5 %reduce-scatter.25.cloned.1.call-done = f32[80,256]{1,0:T(8,128)} async-done(((f32[80,1024]{1,0:T(8,128)}), f32[80,256]{1,0:T(8,128)}) %reduce-scatter.25.cloned.1.call-update) | async-done | bytes 81936 | tf_op jit(solution)/shard_map/reduce_scatter | solution.py:276
  1078.5 25.4 %reduce-scatter.49.cloned.1.call-done = f32[160,256]{1,0:T(8,128)} async-done(((f32[640,256]{1,0:T(8,128)}), f32[160,256]{1,0:T(8,128)}) %reduce-scatter.49.cloned.1.call-update) | async-done | bytes 163856
  1103.9 25.4 %reduce-scatter.39.cloned.1.call-done = f32[80,512]{1,0:T(8,128)} async-done(((f32[80,2048]{1,0:T(8,128)}), f32[80,512]{1,0:T(8,128)}) %reduce-scatter.39.cloned.1.call-update) | async-done | bytes 163856 | tf_op jit(solution)/shard_map/reduce_scatter | solution.py:281
  1129.4 25.6 %reduce-scatter.35.cloned.1.call-done = f32[80,512]{1,0:T(8,128)} async-done(((f32[80,2048]{1,0:T(8,128)}), f32[80,512]{1,0:T(8,128)}) %reduce-scatter.35.cloned.1.call-update) | async-done | bytes 163856 | tf_op jit(solution)/shard_map/reduce_scatter | solution.py:280
  (529 shorter events, 142.2 us)
Async XLA Ops:
  7.2 30.7 %copy-start.149 = (u32[32]{0:T(128)S(1)}, u32[32]{0:T(128)}, u32[]{:S(2)}) copy-start(u32[32]{0:T(128)} %constant.93) | copy-start | bytes 388
  7.2 32.0 %copy-start.156 = (bf16[96]{0:T(256)(128)(2,1)S(1)}, bf16[96]{0:T(256)(128)(2,1)}, u32[]{:S(2)}) copy-start(bf16[96]{0:T(256)(128)(2,1)} %param.20) | copy-start | bytes 580
  7.2 65.8 %copy-start.141 = (bf16[80,64]{0,1:T(8,128)(2,1)S(1)}, bf16[80,64]{0,1:T(8,128)(2,1)}, u32[]{:S(2)}) copy-start(bf16[80,64]{0,1:T(8,128)(2,1)} %param.14) | copy-start | bytes 30724
  7.2 71.2 %copy-start.142 = (bf16[80,64]{0,1:T(8,128)(2,1)S(1)}, bf16[80,64]{0,1:T(8,128)(2,1)}, u32[]{:S(2)}) copy-start(bf16[80,64]{0,1:T(8,128)(2,1)} %param.15) | copy-start | bytes 30724
  7.2 139.8 %copy-start = (bf16[2,512,640]{2,1,0:T(8,128)(2,1)S(1)}, bf16[2,512,640]{2,1,0:T(8,128)(2,1)}, u32[]{:S(2)}) copy-start(bf16[2,512,640]{2,1,0:T(8,128)(2,1)} %param.11) | copy-start | bytes 3932164
  7.2 176.5 %all-gather.7.cloned.1.call-start = ((), (), s32[]{:S(2)}) async-start(), calls=%async_computation.14 | async-start | bytes 1474560 | tf_op jit(solution)/shard_map/all_gather | solution.py:117
  15.9 237.9 %all-gather.9.cloned.1.call-start = ((), (), s32[]{:S(2)}) async-start(), calls=%async_computation.15 | async-start | bytes 1474560 | tf_op jit(solution)/shard_map/all_gather | solution.py:120
  22.3 244.3 %all-gather.11.cloned.1.call-start = ((), (), s32[]{:S(2)}) async-start(), calls=%async_computation.16 | async-start | bytes 2949120 | tf_op jit(solution)/shard_map/all_gather | solution.py:121
  30.4 242.2 %all-gather.13.cloned.1.call-start = ((), (), s32[]{:S(2)}) async-start(), calls=%async_computation.17 | async-start | bytes 2949120 | tf_op jit(solution)/shard_map/all_gather | solution.py:122
  37.8 241.5 %all-gather.15.cloned.1.call-start = ((), (), s32[]{:S(2)}) async-start(), calls=%async_computation.18 | async-start | bytes 2949120 | tf_op jit(solution)/shard_map/all_gather | solution.py:123
  115.2 33.4 %copy-start.52 = (bf16[640,256]{1,0:T(8,128)(2,1)}, bf16[640,256]{1,0:T(8,128)(2,1)S(1)}, u32[]{:S(2)}) copy-start(bf16[640,256]{1,0:T(8,128)(2,1)S(1)} %all_gather.35) | copy-start | bytes 983044
  147.0 12.8 %copy-start.82 = (bf16[640,256]{1,0:T(8,128)(2,1)}, bf16[640,256]{1,0:T(8,128)(2,1)S(1)}, u32[]{:S(2)}) copy-start(bf16[640,256]{1,0:T(8,128)(2,1)S(1)} %all_gather.37) | copy-start | bytes 983044
  147.4 45.5 %copy-start.120 = (f32[512]{0:T(512)}, f32[512]{0:T(512)S(1)}, u32[]{:S(2)}) copy-start(f32[512]{0:T(512)S(1)} %fusion.169) | copy-start | bytes 6148
  147.4 45.5 %copy-start.113 = (f32[640]{0:T(1024)}, f32[640]{0:T(1024)S(1)}, u32[]{:S(2)}) copy-start(f32[640]{0:T(1024)S(1)} %get-tuple-element.155) | copy-start | bytes 7684
  148.0 35.7 %copy-start.122 = (f32[512]{0:T(512)}, f32[512]{0:T(512)S(1)}, u32[]{:S(2)}) copy-start(f32[512]{0:T(512)S(1)} %fusion.164) | copy-start | bytes 6148
  149.7 65.3 %copy-start.128 = (f32[256]{0:T(256)}, f32[256]{0:T(256)S(1)}, u32[]{:S(2)}) copy-start(f32[256]{0:T(256)S(1)} %get-tuple-element.156) | copy-start | bytes 3076
  154.2 7.1 copy-start.91
  154.2 9.8 copy-start.115
  155.0 24.9 %collective-permute-start.2 = (bf16[1,512,512]{1,2,0:T(8,128)(2,1)}, bf16[1,512,512]{1,2,0:T(8,128)(2,1)}, u32[]{:S(2)}, u32[]{:S(2)}) collective-permute-start(bf16[1,512,512]{1,2,0:T(8,128)(2,1)} %pad_maximum_fusion.6), channel_id=1, source_target_pairs={{0,1},{1,2},{2,3},{4,5},{5,6},{6,7},{8,9},{9,10},{10,11},{12,13},{... | collective-permute-start | bytes 1572872 | tf_op jit(solution)/shard_map/ppermute | solution.py:24
  157.1 19.6 %collective-permute-start.1 = (s32[2,512]{1,0:T(2,128)S(1)}, s32[2,512]{1,0:T(2,128)S(1)}, u32[]{:S(2)}, u32[]{:S(2)}) collective-permute-start(s32[2,512]{1,0:T(2,128)S(1)} %copy-done.138), channel_id=1, source_target_pairs={{0,1},{1,2},{2,3},{4,5},{5,6},{6,7},{8,9},{9,10},{10,11},{12,13},{... | collective-permute-start | bytes 12296 | tf_op jit(solution)/shard_map/ppermute | solution.py:24
  161.3 20.6 %collective-permute-start = (bf16[1,512,512]{1,2,0:T(8,128)(2,1)}, bf16[1,512,512]{1,2,0:T(8,128)(2,1)}, u32[]{:S(2)}, u32[]{:S(2)}) collective-permute-start(bf16[1,512,512]{1,2,0:T(8,128)(2,1)} %pad_maximum_fusion.5), channel_id=1, source_target_pairs={{0,1},{1,2},{2,3},{4,5},{5,6},{6,7},{8,9},{9,10},{10,11},{12,13},{... | collective-permute-start | bytes 1572872 | tf_op jit(solution)/shard_map/ppermute | solution.py:24
  170.4 287.4 %reduce-scatter.29.cloned.1.call-start = ((), (), s32[]{:S(2)}) async-start(), calls=%async_computation.22 | async-start | bytes 737280 | tf_op jit(solution)/shard_map/reduce_scatter | solution.py:268
  192.9 22.1 %copy-start.4 = (f32[1,512,4,256]{1,3,2,0:T(8,128)}, f32[1,512,4,256]{1,3,2,0:T(8,128)S(1)}, u32[]{:S(2)}) copy-start(f32[1,512,4,256]{1,3,2,0:T(8,128)S(1)} %copy.156) | copy-start | bytes 6291460
  213.9 11.7 %copy-start.99 = (f32[512,4]{0,1:T(4,128)}, f32[512,4]{0,1:T(4,128)S(1)}, u32[]{:S(2)}) copy-start(f32[512,4]{0,1:T(4,128)S(1)} %fusion.161) | copy-start | bytes 24580
  215.0 12.7 %copy-start.101 = (f32[512,4]{0,1:T(4,128)}, f32[512,4]{0,1:T(4,128)S(1)}, u32[]{:S(2)}) copy-start(f32[512,4]{0,1:T(4,128)S(1)} %fusion.162) | copy-start | bytes 24580
  232.8 6.7 copy-start.43
  232.8 6.7 copy-start.92
  256.3 7.8 copy-start.21
  266.6 19.0 %copy-start.33 = (bf16[512,640]{1,0:T(8,128)(2,1)}, bf16[512,640]{1,0:T(8,128)(2,1)S(1)}, u32[]{:S(2)}) copy-start(bf16[512,640]{1,0:T(8,128)(2,1)S(1)} %get-tuple-element.162) | copy-start | bytes 1966084
  298.3 13.5 %copy-start.73 = (bf16[512,2048]{1,0:T(8,128)(2,1)}, bf16[512,2048]{1,0:T(8,128)(2,1)S(1)}, u32[]{:S(2)}) copy-start(bf16[512,2048]{1,0:T(8,128)(2,1)S(1)} %get-tuple-element.90) | copy-start | bytes 6291460
  318.3 19.8 %copy-start.60 = (bf16[512,640]{1,0:T(8,128)(2,1)}, bf16[512,640]{1,0:T(8,128)(2,1)S(1)}, u32[]{:S(2)}) copy-start(bf16[512,640]{1,0:T(8,128)(2,1)S(1)} %get-tuple-element.158) | copy-start | bytes 1966084
  323.3 7.9 copy-start.90
  331.2 7.0 copy-start.155
  339.7 14.0 %slice-start.2 = ((s8[8388608]{0:T(1024)(128)(4,1)}), s8[4194304]{0:T(1024)(128)(4,1)S(1)}, s32[]{:S(2)}) async-start(s8[8388608]{0:T(1024)(128)(4,1)} %bitcast.466), calls=%async_computation.35 | async-start | bytes 8388608
  346.7 7.0 slice-start.3
  353.7 9.9 slice-start
  353.8 9.8 slice-start.1
  362.3 10.9 collective-permute-start.4
  370.5 7.7 copy-start.37
  371.9 6.2 collective-permute-start.3
  382.8 140.4 %reduce-scatter.27.cloned.1.call-start = ((), (), s32[]{:S(2)}) async-start(), calls=%async_computation.21 | async-start | bytes 737280 | tf_op jit(solution)/shard_map/reduce_scatter | solution.py:267
  389.4 206.7 %reduce-scatter.31.cloned.1.call-start = ((), (), s32[]{:S(2)}) async-start(), calls=%async_computation.23 | async-start | bytes 2949120 | tf_op jit(solution)/shard_map/reduce_scatter | solution.py:269
  393.5 276.2 %reduce-scatter.23.cloned.1.call-start = ((), (), s32[]{:S(2)}) async-start(), calls=%async_computation.19 | async-start | bytes 2949120 | tf_op jit(solution)/shard_map/reduce_scatter | solution.py:266
  409.3 365.3 %reduce-scatter.41.cloned.1.call-start = ((), (), s32[]{:S(2)}) async-start(), calls=%async_computation.28 | async-start | bytes 5898240 | tf_op jit(solution)/shard_map/reduce_scatter | solution.py:272
  418.2 462.4 %reduce-scatter.37.cloned.1.call-start = ((), (), s32[]{:S(2)}) async-start(), calls=%async_computation.26 | async-start | bytes 5898240 | tf_op jit(solution)/shard_map/reduce_scatter | solution.py:271
  426.6 560.0 %reduce-scatter.33.cloned.1.call-start = ((), (), s32[]{:S(2)}) async-start(), calls=%async_computation.24 | async-start | bytes 5898240 | tf_op jit(solution)/shard_map/reduce_scatter | solution.py:270
  434.3 235.5 %copy-start.157 = (u32[32]{0:T(128)S(1)}, u32[32]{0:T(128)}, u32[]{:S(2)}) copy-start(u32[32]{0:T(128)} %constant.99) | copy-start | bytes 388
  434.3 342.5 %copy-start.59 = (bf16[1,512,640]{2,1,0:T(8,128)(2,1)S(1)}, bf16[1,512,640]{2,1,0:T(8,128)(2,1)}, u32[]{:S(2)}) copy-start(bf16[1,512,640]{2,1,0:T(8,128)(2,1)} %get-tuple-element.108) | copy-start | bytes 1966084
  434.4 599.1 %reduce-scatter.45.cloned.1.call-start = ((), (), s32[]{:S(2)}) async-start(), calls=%async_computation.30 | async-start | bytes 163840
  459.5 573.9 %reduce-scatter.43.cloned.1.call-start = ((), (), s32[]{:S(2)}) async-start(), calls=%async_computation.29 | async-start | bytes 163840
  524.8 530.1 %reduce-scatter.47.cloned.1.call-start = ((), (), s32[]{:S(2)}) async-start(), calls=%async_computation.31 | async-start | bytes 409600
  598.1 480.4 %reduce-scatter.25.cloned.1.call-start = ((), (), s32[]{:S(2)}) async-start(), calls=%async_computation.20 | async-start | bytes 409600 | tf_op jit(solution)/shard_map/reduce_scatter | solution.py:276
  669.7 434.2 %reduce-scatter.49.cloned.1.call-start = ((), (), s32[]{:S(2)}) async-start(), calls=%async_computation.32 | async-start | bytes 819200
  671.7 107.5 %copy-start.40 = (bf16[640,1024]{1,0:T(8,128)(2,1)S(1)}, bf16[640,1024]{1,0:T(8,128)(2,1)}, u32[]{:S(2)}) copy-start(bf16[640,1024]{1,0:T(8,128)(2,1)} %all-gather.7.cloned.1.call-done) | copy-start | bytes 3932164
  776.8 352.6 %reduce-scatter.39.cloned.1.call-start = ((), (), s32[]{:S(2)}) async-start(), calls=%async_computation.27 | async-start | bytes 819200 | tf_op jit(solution)/shard_map/reduce_scatter | solution.py:281
  783.0 97.8 %copy-start.83 = (bf16[640,256]{1,0:T(8,128)(2,1)S(1)}, bf16[640,256]{1,0:T(8,128)(2,1)}, u32[]{:S(2)}) copy-start(bf16[640,256]{1,0:T(8,128)(2,1)} %copy-done.82) | copy-start | bytes 983044
  783.0 97.8 %copy-start.85 = (bf16[512,256]{0,1:T(8,128)(2,1)S(1)}, bf16[512,256]{0,1:T(8,128)(2,1)}, u32[]{:S(2)}) copy-start(bf16[512,256]{0,1:T(8,128)(2,1)} %copy-done.84) | copy-start | bytes 786436
  783.4 97.8 %copy-start.87 = (bf16[512,256]{0,1:T(8,128)(2,1)S(1)}, bf16[512,256]{0,1:T(8,128)(2,1)}, u32[]{:S(2)}) copy-start(bf16[512,256]{0,1:T(8,128)(2,1)} %copy-done.86) | copy-start | bytes 786436
  880.7 274.3 %reduce-scatter.35.cloned.1.call-start = ((), (), s32[]{:S(2)}) async-start(), calls=%async_computation.25 | async-start | bytes 819200 | tf_op jit(solution)/shard_map/reduce_scatter | solution.py:280
  882.1 104.5 %copy-start.139 = (f32[640]{0:T(1024)S(1)}, f32[640]{0:T(1024)}, u32[]{:S(2)}) copy-start(f32[640]{0:T(1024)} %get-tuple-element.62) | copy-start | bytes 7684
  882.1 104.5 %copy-start.140 = (f32[640]{0:T(1024)S(1)}, f32[640]{0:T(1024)}, u32[]{:S(2)}) copy-start(f32[640]{0:T(1024)} %get-tuple-element.73) | copy-start | bytes 7684
  882.1 146.8 %copy-start.133 = (f32[512]{0:T(512)S(1)}, f32[512]{0:T(512)}, u32[]{:S(2)}) copy-start(f32[512]{0:T(512)} %copy-done.132) | copy-start | bytes 6148
  882.1 146.8 %copy-start.135 = (f32[512]{0:T(512)S(1)}, f32[512]{0:T(512)}, u32[]{:S(2)}) copy-start(f32[512]{0:T(512)} %copy-done.134) | copy-start | bytes 6148
  882.1 146.8 %copy-start.19 = (f32[512,640]{1,0:T(8,128)S(1)}, f32[512,640]{1,0:T(8,128)}, u32[]{:S(2)}) copy-start(f32[512,640]{1,0:T(8,128)} %copy-done.18) | copy-start | bytes 3932164
  (125 other events, 348.0 us)
Sparse Core Ops, SparseCore 0:
  16.0 42.2 all-gather.6
  60.4 43.0 all-gather.8
  105.7 55.6 all-gather.10
  163.4 53.3 all-gather.12
  218.8 55.4 all-gather.14
  382.9 74.8 reduce-scatter.28
  462.0 61.0 reduce-scatter.26
  526.7 69.4 reduce-scatter.30
  600.3 69.3 reduce-scatter.22
  673.1 101.4 reduce-scatter.40
  778.2 102.4 reduce-scatter.36
  884.1 102.4 reduce-scatter.32
  989.6 19.2 reduce-scatter.44
  1011.9 19.5 reduce-scatter.42
  1034.5 20.4 reduce-scatter.46
  1058.0 20.4 reduce-scatter.24
  1081.4 22.4 reduce-scatter.48
  1106.9 22.4 reduce-scatter.38
  1132.5 22.4 reduce-scatter.34
where the time goes:
time: 1170 us; the launch traced here: 1160 us
  waiting for transfers between devices  656 us (56%)
  blocking collectives  186 us (16%)
  matrix products  144 us (12%)
  local copies, waits for them, and re-layouts  76.3 us (7%)
  other arithmetic  69.2 us (6%)
  between operations  18.9 us (2%)
    reduce_scatter x1, waiting for transfers between devices, local(): lax.psum_scatter(grad_down, 'dp', scatter_dimension=0, tiled=True)  103 us
    reduce_scatter x1, waiting for transfers between devices, local(): lax.psum_scatter(grad_gate, 'dp', scatter_dimension=0, tiled=True)  102 us
    reduce_scatter x1, waiting for transfers between devices, local(): lax.psum_scatter(grad_up, 'dp', scatter_dimension=0, tiled=True)  97.2 us
    reduce_scatter x1, waiting for transfers between devices, local(): lax.psum_scatter(grad_query, 'dp', scatter_dimension=0, tiled=True)  71.6 us
    reduce_scatter x1, waiting for transfers between devices, local(): lax.psum_scatter(grad_out, 'dp', scatter_dimension=0, tiled=True)  71.3 us
    reduce_scatter x1, waiting for transfers between devices, local(): lax.psum_scatter(grad_key, 'dp', scatter_dimension=0, tiled=True)  63.6 us
    unnamed x3, blocking collectives  48.5 us
    unnamed x23, waiting for transfers between devices  47.3 us
  transfers between devices with their start and end apart: 24, of which 13 were waited for; matrix products, arithmetic and copies ran while one was open for 16% of the time, Pallas kernels for 0%

commit v1 on v0

--- a/solution.py
+++ b/solution.py
@@ -11,7 +11,7 @@
 HD = 256
 FF = 2048
 WINDOW = 512
-MICRO = 2
+MICRO = 1
 
 
 EPSILON = 1e-06
@@ -102,42 +102,69 @@
     reach = (distance >= 0) & (distance < WINDOW) & ((col_index >= block_len) | (seq_place > 0))
     allowed_all = reach[None] & (segment_ids[:, :, None] == key_ids[:, None, :])
 
+    dp_size = lax.axis_size("dp")
+    seq_size = lax.axis_size("seq")
+
+    def gathered(block):
+        stacked = lax.all_gather(block, "dp", axis=0, tiled=False)
+        return lax.all_gather(stacked, "seq", axis=0, tiled=False)
+
+    def columns_joined(stack):
+        return stack.transpose(1, 2, 0, 3).reshape(dp_size * stack.shape[2], -1)
+
+    def rows_joined(stack):
+        return stack.transpose(0, 2, 1, 3).reshape(seq_size * stack.shape[2], -1)
+
     def fetch_weights():
-        halfway = (
-            lax.all_gather(query_weight, "seq", axis=1, tiled=True),
-            lax.all_gather(key_weight, "seq", axis=1, tiled=True),
-            lax.all_gather(value_weight, "seq", axis=1, tiled=True),
-            lax.all_gather(out_weight, "seq", axis=1, tiled=True),
-            lax.all_gather(gate_weight, "seq", axis=1, tiled=True),
-            lax.all_gather(up_weight, "seq", axis=1, tiled=True),
-            lax.all_gather(down_weight, "seq", axis=1, tiled=True),
-            lax.all_gather(norm_gains, "seq", axis=0, tiled=True),
-        )
+        rows_in = query_weight.shape[0]
+        query_cols = query_weight.shape[1]
+        key_cols = key_weight.shape[1]
+        width = query_cols + 2 * key_cols
+        gain_rows = -(-norm_gains.shape[0] // width)
+        gain_rows = -(-gain_rows // 16) * 16
+        gain_block = jnp.pad(norm_gains, (0, gain_rows * width - norm_gains.shape[0])).reshape(
+            gain_rows, width
+        )
+        first = jnp.concatenate(
+            [jnp.concatenate([query_weight, key_weight, value_weight], axis=1), gain_block], axis=0
+        )
+        first = gathered(first)
+        second = gathered(out_weight.T)
+        third = gathered(jnp.concatenate([gate_weight, up_weight], axis=1))
+        fourth = gathered(down_weight.T)
+        half = gate_weight.shape[1]
+        gains_all = first[:, :, rows_in:].reshape(seq_size, dp_size, -1)[..., : norm_gains.shape[0]]
         return (
-            lax.all_gather(halfway[0], "dp", axis=0, tiled=True),
-            lax.all_gather(halfway[1], "dp", axis=0, tiled=True),
-            lax.all_gather(halfway[2], "dp", axis=0, tiled=True),
-            lax.all_gather(halfway[3], "dp", axis=0, tiled=True),
-            lax.all_gather(halfway[4], "dp", axis=0, tiled=True),
-            lax.all_gather(halfway[5], "dp", axis=0, tiled=True),
-            lax.all_gather(halfway[6], "dp", axis=0, tiled=True),
-            lax.all_gather(halfway[7], "dp", axis=0, tiled=True),
-        )
-
-    grad_query = jnp.zeros((D, NQ * HD), jnp.float32)
-    grad_key = jnp.zeros((D, HD), jnp.float32)
-    grad_value = jnp.zeros((D, HD), jnp.float32)
-    grad_out = jnp.zeros((NQ * HD, D), jnp.float32)
-    grad_gate = jnp.zeros((D, FF), jnp.float32)
-    grad_up = jnp.zeros((D, FF), jnp.float32)
-    grad_down = jnp.zeros((FF, D), jnp.float32)
-    grad_gains = jnp.zeros((4 * D + 2 * HD,), jnp.float32)
+            columns_joined(first[:, :, :rows_in, :query_cols]),
+            columns_joined(first[:, :, :rows_in, query_cols : query_cols + key_cols]),
+            columns_joined(first[:, :, :rows_in, query_cols + key_cols :]),
+            rows_joined(second),
+            columns_joined(third[..., :half]),
+            columns_joined(third[..., half:]),
+            rows_joined(fourth),
+            gains_all.transpose(1, 0, 2).reshape(-1),
+        )
+
+    weights_all = fetch_weights()
+
+    def seq_summed(block):
+        return lax.psum_scatter(block, "seq", scatter_dimension=0, tiled=True)
+
+    def dp_summed(block):
+        return lax.psum_scatter(block, "dp", scatter_dimension=0, tiled=True)
+
+    def seq_split(block):
+        return block.astype(jnp.bfloat16).reshape(seq_size, -1, block.shape[1])
+
+    def dp_split(block):
+        return block.reshape(block.shape[0], dp_size, -1).transpose(1, 0, 2)
+
     out_blocks = []
     grad_blocks = []
     for micro_index in range(MICRO):
         row_lower = micro_index * per_batch
         row_upper = row_lower + per_batch
-        weights_now = fetch_weights()
+        weights_now = weights_all
         gains_float = weights_now[7].astype(jnp.float32)
         in_scale = gains_float[0:D]
         attn_scale = gains_float[D : 2 * D]
@@ -179,7 +206,7 @@
             "shqk,skd->sqhd", prob_weights, values_all, preferred_element_type=jnp.float32
         )
         mixed_heads = mixed_heads.astype(jnp.bfloat16).reshape(token_count, NQ * HD)
-        branch = plain_product(mixed_heads, weights_now[3])
+        branch = times_transposed(mixed_heads, weights_now[3])
         post_vals, post_pull = jax.vjp(rms_scale, branch, attn_scale)
         residual = tokens_now + post_vals
         inner_vals, inner_pull = jax.vjp(rms_scale, residual, pre_scale)
@@ -188,22 +215,29 @@
         up_vals = plain_product(inner_normed, weights_now[5])
         hidden_vals, hidden_pull = jax.vjp(gated_inner, gate_vals, up_vals)
         hidden = hidden_vals.astype(jnp.bfloat16)
-        ffn_vals = plain_product(hidden, weights_now[6])
+        ffn_vals = times_transposed(hidden, weights_now[6])
         final_vals, final_pull = jax.vjp(rms_scale, ffn_vals, post_scale)
         out_blocks.append(
             (residual + final_vals).astype(jnp.bfloat16).reshape(per_batch, block_len, D)
         )
-        weights_back = fetch_weights()
+        weights_back = weights_all
         cotangent = d_output[row_lower:row_upper].astype(jnp.float32).reshape(token_count, D)
         d_ffn, d_post_scale = final_pull(cotangent)
         d_ffn = d_ffn.astype(jnp.bfloat16)
-        grad_down = grad_down + rows_product(hidden, d_ffn)
-        d_hidden = times_transposed(d_ffn, weights_back[6])
+        grad_down = seq_summed(rows_product(d_ffn, hidden).astype(jnp.bfloat16))
+        d_hidden = plain_product(d_ffn, weights_back[6])
         d_gate, d_up = hidden_pull(d_hidden)
         d_gate = d_gate.astype(jnp.bfloat16)
         d_up = d_up.astype(jnp.bfloat16)
-        grad_gate = grad_gate + rows_product(inner_normed, d_gate)
-        grad_up = grad_up + rows_product(inner_normed, d_up)
+        grad_pair = seq_summed(
+            jnp.concatenate(
+                [
+                    seq_split(rows_product(d_gate, inner_normed)),
+                    seq_split(rows_product(d_up, inner_normed)),
+                ],
+                axis=1,
+            )
+        )[0]
         d_inner = times_transposed(d_gate, weights_back[4]) + times_transposed(
             d_up, weights_back[5]
         )
@@ -211,9 +245,9 @@
         d_resid = cotangent + d_resid_part
         d_branch, d_attn_scale = post_pull(d_resid)
         d_branch = d_branch.astype(jnp.bfloat16)
-        grad_out = grad_out + rows_product(mixed_heads, d_branch)
+        grad_out = seq_summed(rows_product(d_branch, mixed_heads).astype(jnp.bfloat16))
         d_mixed = (
-            times_transposed(d_branch, weights_back[3])
+            plain_product(d_branch, weights_back[3])
             .astype(jnp.bfloat16)
             .reshape(per_batch, block_len, NQ, HD)
         )
@@ -235,7 +269,7 @@
         d_values = jnp.einsum(
             "shqk,sqhd->skd", probs_again, d_mixed, preferred_element_type=jnp.float32
         )
-        earlier_part = jnp.concatenate([d_keys[:, :block_len], d_values[:, :block_len]], axis=-1)
+        earlier_part = jnp.concatenate([d_keys[:, :block_len], d_values[:, :block_len]], axis=-1).astype(jnp.bfloat16)
         later_pair = shifted(earlier_part, "seq", -1)
         d_keys_own = d_keys[:, block_len:] + later_pair[..., :HD]
         d_values_own = (
@@ -247,9 +281,9 @@
         d_query_raw = d_query_raw.astype(jnp.bfloat16).reshape(token_count, NQ * HD)
         d_key_raw, d_key_scale = key_pull(d_keys_own)
         d_key_raw = d_key_raw.astype(jnp.bfloat16).reshape(token_count, HD)
-        grad_query = grad_query + rows_product(normed, d_query_raw)
-        grad_key = grad_key + rows_product(normed, d_key_raw)
-        grad_value = grad_value + rows_product(normed, d_values_own)
+        grad_query = rows_product(d_query_raw, normed)
+        grad_key = rows_product(d_key_raw, normed)
+        grad_value = rows_product(d_values_own, normed)
         d_normed = (
             times_transposed(d_query_raw, weights_back[0])
             + times_transposed(d_key_raw, weights_back[1])
@@ -257,43 +291,58 @@
         )
         d_tokens, d_in_scale = input_pull(d_normed)
         grad_blocks.append((d_resid + d_tokens).reshape(per_batch, block_len, D))
-        grad_gains = grad_gains + jnp.concatenate(
+        grad_gains = jnp.concatenate(
             [d_in_scale, d_attn_scale, d_pre_scale, d_post_scale, d_query_scale, d_key_scale]
         )
     output = jnp.concatenate(out_blocks, axis=0)
     grad_input = jnp.concatenate(grad_blocks, axis=0)
-    reduced_dp = (
-        lax.psum_scatter(grad_query, "dp", scatter_dimension=0, tiled=True),
-        lax.psum_scatter(grad_key, "dp", scatter_dimension=0, tiled=True),
-        lax.psum_scatter(grad_value, "dp", scatter_dimension=0, tiled=True),
-        lax.psum_scatter(grad_out, "dp", scatter_dimension=0, tiled=True),
-        lax.psum_scatter(grad_gate, "dp", scatter_dimension=0, tiled=True),
-        lax.psum_scatter(grad_up, "dp", scatter_dimension=0, tiled=True),
-        lax.psum_scatter(grad_down, "dp", scatter_dimension=0, tiled=True),
-        lax.psum_scatter(grad_gains, "dp", scatter_dimension=0, tiled=True),
-    )
-    reduced = (
-        lax.psum_scatter(reduced_dp[0], "seq", scatter_dimension=1, tiled=True),
-        lax.psum_scatter(reduced_dp[1], "seq", scatter_dimension=1, tiled=True),
-        lax.psum_scatter(reduced_dp[2], "seq", scatter_dimension=1, tiled=True),
-        lax.psum_scatter(reduced_dp[3], "seq", scatter_dimension=1, tiled=True),
-        lax.psum_scatter(reduced_dp[4], "seq", scatter_dimension=1, tiled=True),
-        lax.psum_scatter(reduced_dp[5], "seq", scatter_dimension=1, tiled=True),
-        lax.psum_scatter(reduced_dp[6], "seq", scatter_dimension=1, tiled=True),
-        lax.psum_scatter(reduced_dp[7], "seq", scatter_dimension=0, tiled=True),
-    )
-    gains_done = reduced[7]
+    gain_count = norm_gains.shape[0]
+    gain_rows = -(-(dp_size * gain_count) // (16 * D)) * 16
+    gain_part = grad_gains.reshape(dp_size, seq_size, gain_count).transpose(1, 0, 2)
+    gain_part = jnp.pad(
+        gain_part.reshape(seq_size, -1), ((0, 0), (0, gain_rows * D - dp_size * gain_count))
+    ).reshape(seq_size, gain_rows, D)
+    last = seq_summed(
+        jnp.concatenate(
+            [
+                seq_split(grad_query),
+                seq_split(grad_key),
+                seq_split(grad_value),
+                gain_part.astype(jnp.bfloat16),
+            ],
+            axis=1,
+        )
+    )[0]
+    width = last.shape[0] - gain_rows
+    gain_now = last[width:].reshape(-1)[: dp_size * gain_count].reshape(dp_size, gain_count)
+    extra = -(-gain_count // (16 * width)) * 16
+    gain_now = jnp.pad(gain_now, ((0, 0), (0, extra * width - gain_count)))
+    last = jnp.concatenate(
+        [
+            last[:width].T.reshape(dp_size, D // dp_size, width),
+            gain_now.reshape(dp_size, extra, width),
+        ],
+        axis=1,
+    )
+    last = dp_summed(last)[0].astype(jnp.float32)
+    rows_in = query_weight.shape[0]
+    query_cols = query_weight.shape[1]
+    key_cols = key_weight.shape[1]
+    half = gate_weight.shape[1]
+    pair_done = dp_summed(grad_pair.T).astype(jnp.float32)
+    out_done = dp_summed(dp_split(grad_out))[0].astype(jnp.float32).T
+    down_done = dp_summed(dp_split(grad_down))[0].astype(jnp.float32).T
     return (
         output,
         grad_input,
-        reduced[0],
-        reduced[1],
-        reduced[2],
-        reduced[3],
-        reduced[4],
-        reduced[5],
-        reduced[6],
-        gains_done,
+        last[:rows_in, :query_cols],
+        last[:rows_in, query_cols : query_cols + key_cols],
+        last[:rows_in, query_cols + key_cols :],
+        out_done,
+        pair_done[:, :half],
+        pair_done[:, half:],
+        down_done,
+        last[rows_in:].reshape(-1)[:gain_count],
     )
 
 

time: 1170 us -> 760 us (0.65)
  waiting for transfers between devices: 656 us -> 336 us
  blocking collectives: 186 us -> 104 us
  local copies, waits for them, and re-layouts: 76.3 us -> 92.9 us
  matrix products: 144 us -> 131 us
    reduce_scatter x10 -> x8, waiting for transfers between devices: 607 us -> 333 us  [the longest x4 248 us: dp_summed(): return lax.psum_scatter(block, 'dp', scatter_dimension=0, tiled=True)]
    unnamed x3 -> x0, blocking collectives: 48.5 us -> none
    unnamed x23 -> x13, waiting for transfers between devices: 47.3 us -> 0.22 us
    all_gather x10 -> x3, blocking collectives: 137 us -> 104 us  [gathered(): stacked = lax.all_gather(block, 'dp', axis=0, tiled=False)]
    transpose x0 -> x12, local copies, waits for them, and re-layouts: none -> 22.7 us  [the longest x8 13.8 us: columns_joined(): return stack.transpose(1, 2, 0, 3).reshape(dp_size * stack.shape[2], -1)]
    convert_element_type x0 -> x6, other arithmetic: none -> 16.6 us  [the longest x1 11.7 us: local(): d_scores = (probs_float * (d_probs - row_inner)).astype(jnp.bfloat16)]
    unnamed x350 -> x170, local copies, waits for them, and re-layouts: 34.8 us -> 20.9 us
    reshape x6 -> x16, local copies, waits for them, and re-layouts: 15.8 us -> 24.2 us  [the longest x5 13.6 us: seq_split(): return block.astype(jnp.bfloat16).reshape(seq_size, -1, block.shape[1])]
  transfers between devices with their start and end apart: 24 -> 16, of which waited for: 13 -> 7; matrix products, arithmetic and copies ran while one was open for 16% -> 24% of each run, Pallas kernels for 0% -> 0%
where the time goes in v1:
time: 760 us; the launch traced here: 751 us
  waiting for transfers between devices  336 us (44%)
  matrix products  131 us (17%)
  blocking collectives  104 us (14%)
  local copies, waits for them, and re-layouts  92.9 us (12%)
  other arithmetic  64.3 us (8%)
  between operations  15.7 us (2%)
    reduce_scatter x4, waiting for transfers between devices, dp_summed(): return lax.psum_scatter(block, 'dp', scatter_dimension=0, tiled=True)  248 us
    all_gather x3, blocking collectives, gathered(): stacked = lax.all_gather(block, 'dp', axis=0, tiled=False)  104 us
    reduce_scatter x4, waiting for transfers between devices, seq_summed(): return lax.psum_scatter(block, 'seq', scatter_dimension=0, tiled=True)  84.7 us
    dot_general x7, matrix products, rows_product(): lax.dot_general(left_side, right_side, (((0,), (0,)), ((), ())), preferre...  32.9 us
    dot_general x7, matrix products, plain_product(): return jnp.dot(left_side, right_side, preferred_element_type=jnp.float32)  32.6 us
    dot_general x7, matrix products, times_transposed(): lax.dot_general(left_side, right_side, (((1,), (1,)), ((), ())), preferre...  22.3 us
    unnamed x170, local copies, waits for them, and re-layouts  20.9 us
  transfers between devices with their start and end apart: 16, of which 7 were waited for; matrix products, arithmetic and copies ran while one was open for 24% of the time, Pallas kernels for 0%

profile of v1, /device:TPU:0, one launch (start us, length us, event | category | flops | bytes accessed | tf_op | source)
XLA Modules:
  0.0 750.9 jit_solution(18006877757386214831)
XLA Ops:
  7.3 35.0 %all-gather.2 = bf16[1280,128]{1,0:T(8,128)(2,1)} all-gather(bf16[160,128]{1,0:T(8,128)(2,1)} %bitcast.330), channel_id=4, replica_groups=mesh['dp'=8,'seq'=4] {'dp'}, dimensions={0}, use_global_device_ids=true | all-gather | bytes 368640 | tf_op jit(solution)/shard_map/all_gather | solution.py:109
  47.2 34.4 %all-gather = bf16[768,384]{1,0:T(8,128)(2,1)} all-gather(bf16[96,384]{1,0:T(8,128)(2,1)S(1)} %pad_maximum_fusion.7), channel_id=2, replica_groups=mesh['dp'=8,'seq'=4] {'dp'}, dimensions={0}, use_global_device_ids=true | all-gather | bytes 663552 | tf_op jit(solution)/shard_map/all_gather | solution.py:109
  81.7 34.4 %all-gather.6 = bf16[1280,256]{1,0:T(8,128)(2,1)} all-gather(bf16[160,256]{1,0:T(8,128)(2,1)S(1)} %bitcast.329), channel_id=8, replica_groups=mesh['dp'=8,'seq'=4] {'dp'}, dimensions={0}, use_global_device_ids=true | all-gather | bytes 737280 | tf_op jit(solution)/shard_map/all_gather | solution.py:109
  118.6 2.8 broadcast_multiply_fusion.1
  124.7 2.1 copy.136
  129.5 2.8 copy.128
  132.5 2.6 all-gather.14.cloned.1.call-done
  136.8 2.5 slice_bitcast_fusion.4
  139.3 1.9 reshape.504
  142.1 2.2 copy.117
  150.9 2.0 convolution_convert_fusion.6
  155.8 3.2 collective-permute-start
  160.4 1.9 copy.121
  162.3 3.2 multiply_reduce_fusion.2
  169.6 4.2 copy.131
  173.8 2.4 copy.180
  176.2 2.1 fusion.92
  178.3 10.2 %fusion.97 = (f32[2,4,512]{2,1,0:T(4,128)S(1)}, f32[2,4,512,1024]{2,3,1,0:T(8,128)}) fusion(pred[2,512,1024]{1,2,0:T(8,128)(4,1)} %compare_and_fusion, bf16[2,512,4,256]{1,3,2,0:T(8,128)(2,1)S(1)} %fusion.17, bf16[2,512,256]{2,1,0:T(8,128)(2,1)S(1)} %fusion.65, bf16[2,512,256]{2,1,0:T(8,128)(2,1)S(1)} %get-tuple-element.83), kind=kOutput, calls=%fused_computation.200 | convolution fusion | flops 2162164736 | bytes 20987904 | tf_op jit(solution)/shard_map/sub | solution.py:202
  188.5 9.9 %convert_bitcast_fusion = bf16[2,512,4,256]{1,3,2,0:T(8,128)(2,1)} fusion(bf16[2,512,256]{2,1,0:T(8,128)(2,1)} %bitcast.321, bf16[2,512,256]{2,1,0:T(8,128)(2,1)} %get-tuple-element.84, f32[2,4,512,1024]{2,3,1,0:T(8,128)} %get-tuple-element.108, f32[2,4,512]{2,1,0:T(4,128)S(1)} %get-tuple-element.107), kind=kOutput, calls=%fused_computation.89 | convolution fusion | flops 2159017984 | bytes 19939328 | tf_op jit(solution)/shard_map/shqk,skd->sqhd/dot_general | solution.py:205
  198.4 3.2 copy.127
  202.9 2.0 multiply_reduce_fusion.9
  207.9 2.9 slice_bitcast_fusion.1
  210.8 2.0 copy.129
  213.6 2.0 copy.130
  217.0 3.4 fusion.98
  220.4 7.2 multiply_convert_fusion.1
  227.7 3.6 multiply_reduce_fusion.7
  232.3 2.2 fusion.29
  234.5 12.8 %multiply_convert_fusion = (bf16[1024,2048]{1,0:T(8,128)(2,1)}, bf16[1024,2048]{1,0:T(8,128)(2,1)}) fusion(f32[1024,2048]{1,0:T(8,128)S(1)} %fusion.98, f32[1024,2048]{1,0:T(8,128)} %get-tuple-element.112, bf16[1024,640]{1,0:T(8,128)(2,1)S(1)} %get-tuple-element.75, bf16[640,2048]{1,0:T(8,128)(2,1)S(1)} %bitcast.293), kind=kOutput, calls=%fused_computation.18 | convolution fusion | flops 2734686208 | bytes 29097984 | tf_op jit(solution)/shard_map/dot_general | solution.py:74
  247.3 6.0 fusion.99
  253.3 3.8 multiply_reduce_fusion.3
  257.2 1.9 multiply_reduce_fusion.4
  261.7 3.1 convolution_convert_fusion.3
  264.8 3.3 reshape.517
  268.2 7.2 fusion.48
  275.3 11.3 %fusion.1 = (f32[2,4,512]{2,1,0:T(4,128)S(1)}, f32[2,1024,512,4]{2,1,3,0:T(8,128)}) fusion(f32[2,4,512,1024]{2,3,1,0:T(8,128)} %get-tuple-element.108, f32[2,4,512]{2,1,0:T(4,128)S(1)} %get-tuple-element.107, bf16[2,512,4,256]{3,2,1,0:T(4,128)(2,1)S(1)} %reshape.517, bf16[2,512,256]{2,1,0:T(8,128)(2,1)S(1)} %bitcast.322, bf16[2,512,256]{2,1,0:T(8,128)(2,1)S(1)} %copy-done.53), kind=kOutput, calls=%fused_computation.3 | convolution fusion | flops 2162159616 | bytes 36732928 | tf_op jit(solution)/shard_map/sqhd,skd->shqk/dot_general | solution.py:260
  286.7 11.7 %fusion.3 = bf16[2,4,512,1024]{2,3,1,0:T(8,128)(2,1)S(1)} fusion(f32[2,1024,512,4]{2,1,3,0:T(8,128)} %get-tuple-element.117, f32[2,4,512]{2,1,0:T(4,128)S(1)} %get-tuple-element.116, f32[2,4,512,1024]{2,3,1,0:T(8,128)} %get-tuple-element.108, f32[2,4,512]{2,1,0:T(4,128)S(1)} %get-tuple-element.107), kind=kLoop, calls=%fused_computation.5 | loop fusion | flops 16777216 | bytes 41975808 | tf_op jit(solution)/shard_map/convert_element_type | solution.py:264
  298.4 2.4 convolution_bitcast_fusion
  303.6 2.5 bitcast_multiply_fusion.1
  308.4 2.0 multiply_reduce_fusion
  310.5 2.6 fusion.14
  313.0 3.0 copy.137
  317.4 1.9 convolution_convert_fusion.5
  320.8 4.7 convolution_convert_fusion.4
  325.8 3.6 fusion.100
  334.9 2.7 fusion.38
  339.4 2.4 fusion.59
  341.7 2.1 copy.145
  343.8 2.4 fusion.58
  347.5 3.8 pad_maximum_fusion.1
  352.6 6.7 convolution_convert_fusion
  360.7 7.3 convolution_convert_fusion.1
  368.0 4.4 copy.150
  372.4 7.6 %convolution_convert_fusion.2 = bf16[2048,640]{1,0:T(8,128)(2,1)} fusion(bf16[1024,2048]{1,0:T(8,128)(2,1)} %get-tuple-element.68, bf16[1024,640]{1,0:T(8,128)(2,1)S(1)} %copy-done.47), kind=kOutput, calls=%fused_computation.53 | convolution fusion | flops 2685665280 | bytes 8126464 | tf_op jit(solution)/shard_map/dot_general | solution.py:62
  379.9 4.4 copy.149
  384.3 5.6 pad_maximum_fusion
  395.2 32.7 %reduce-scatter.21.cloned.1.call-done = bf16[160,2048]{1,0:T(8,128)(2,1)} async-done(((bf16[640,2048]{1,0:T(8,128)(2,1)}), bf16[160,2048]{1,0:T(8,128)(2,1)}) %reduce-scatter.21.cloned.1.call-update) | async-done | bytes 655376 | tf_op jit(solution)/shard_map/reduce_scatter | solution.py:151
  427.9 2.1 copy.207
  430.0 52.0 %reduce-scatter.17.cloned.1.call-done = bf16[1,1024,640]{1,2,0:T(8,128)(2,1)} async-done(((bf16[4,1024,640]{1,2,0:T(8,128)(2,1)}), bf16[1,1024,640]{1,2,0:T(8,128)(2,1)}) %reduce-scatter.17.cloned.1.call-update) | async-done | bytes 1310736 | tf_op jit(solution)/shard_map/reduce_scatter | solution.py:151
  482.0 4.7 fusion.31
  486.7 59.8 %reduce-scatter.15.cloned.1.call-done = bf16[1,160,128]{2,1,0:T(8,128)(2,1)} async-done(((bf16[8,160,128]{2,1,0:T(8,128)(2,1)}), bf16[1,160,128]{2,1,0:T(8,128)(2,1)}) %reduce-scatter.15.cloned.1.call-update) | async-done | bytes 40976 | tf_op jit(solution)/shard_map/reduce_scatter | solution.py:154
  547.9 63.0 %reduce-scatter.11.cloned.1.call-done = bf16[1,96,384]{2,1,0:T(8,128)(2,1)} async-done(((bf16[8,96,384]{2,1,0:T(8,128)(2,1)}), bf16[1,96,384]{2,1,0:T(8,128)(2,1)}) %reduce-scatter.11.cloned.1.call-update) | async-done | bytes 73744 | tf_op jit(solution)/shard_map/reduce_scatter | solution.py:154
  615.2 60.3 %reduce-scatter.23.cloned.1.call-done = bf16[1,160,256]{2,1,0:T(8,128)(2,1)} async-done(((bf16[8,160,256]{2,1,0:T(8,128)(2,1)}), bf16[1,160,256]{2,1,0:T(8,128)(2,1)}) %reduce-scatter.23.cloned.1.call-update) | async-done | bytes 81936 | tf_op jit(solution)/shard_map/reduce_scatter | solution.py:154
  677.0 65.3 %reduce-scatter.19.cloned.1.call-done = bf16[80,1024]{1,0:T(8,128)(2,1)} async-done(((bf16[640,1024]{1,0:T(8,128)(2,1)}), bf16[80,1024]{1,0:T(8,128)(2,1)}) %reduce-scatter.19.cloned.1.call-update) | async-done | bytes 163856 | tf_op jit(solution)/shard_map/reduce_scatter | solution.py:154
  (295 shorter events, 74.0 us)
Async XLA Ops:
  7.2 74.5 %copy-start.58 = (bf16[256,160]{0,1:T(8,128)(2,1)S(1)}, bf16[256,160]{0,1:T(8,128)(2,1)}, u32[]{:S(2)}) copy-start(bf16[256,160]{0,1:T(8,128)(2,1)} %param.19) | copy-start | bytes 245764
  7.2 108.9 %copy-start.72 = (s32[2,512]{1,0:T(2,128)S(1)}, s32[2,512]{1,0:T(2,128)}, u32[]{:S(2)}) copy-start(s32[2,512]{1,0:T(2,128)} %param.12) | copy-start | bytes 12292
  7.2 110.3 %copy-start.2 = (bf16[2,512,640]{2,1,0:T(8,128)(2,1)S(1)}, bf16[2,512,640]{2,1,0:T(8,128)(2,1)}, u32[]{:S(2)}) copy-start(bf16[2,512,640]{2,1,0:T(8,128)(2,1)} %param.11) | copy-start | bytes 3932164
  7.2 122.3 %all-gather.16.cloned.1.call-start = ((), (), s32[]{:S(2)}) async-start(), calls=%async_computation.17 | async-start | bytes 1638400 | tf_op jit(solution)/shard_map/all_gather | solution.py:110
  42.3 90.1 %all-gather.18.cloned.1.call-start = ((), (), s32[]{:S(2)}) async-start(), calls=%async_computation.18 | async-start | bytes 1474560 | tf_op jit(solution)/shard_map/all_gather | solution.py:109
  43.9 91.1 %all-gather.14.cloned.1.call-start = ((), (), s32[]{:S(2)}) async-start(), calls=%async_computation.16 | async-start | bytes 2949120 | tf_op jit(solution)/shard_map/all_gather | solution.py:110
  81.6 88.0 %all-gather.22.cloned.1.call-start = ((), (), s32[]{:S(2)}) async-start(), calls=%async_computation.20 | async-start | bytes 3276800 | tf_op jit(solution)/shard_map/all_gather | solution.py:110
  116.1 91.8 %all-gather.20.cloned.1.call-start = ((), (), s32[]{:S(2)}) async-start(), calls=%async_computation.19 | async-start | bytes 6553600 | tf_op jit(solution)/shard_map/all_gather | solution.py:110
  116.1 11.7 %collective-permute-start.1 = (s32[2,512]{1,0:T(2,128)S(1)}, s32[2,512]{1,0:T(2,128)S(1)}, u32[]{:S(2)}, u32[]{:S(2)}) collective-permute-start(s32[2,512]{1,0:T(2,128)S(1)} %copy-done.72), channel_id=1, source_target_pairs={{0,1},{1,2},{2,3},{4,5},{5,6},{6,7},{8,9},{9,10},{10,11},{12,13},{... | collective-permute-start | bytes 12296 | tf_op jit(solution)/shard_map/ppermute | solution.py:24
  121.3 31.6 %copy-start.11 = (f32[512,256]{1,0:T(8,128)}, f32[512,256]{1,0:T(8,128)S(1)}, u32[]{:S(2)}) copy-start(f32[512,256]{1,0:T(8,128)S(1)} %get-tuple-element.90) | copy-start | bytes 1572868
  121.3 31.6 %copy-start.13 = (f32[512,256]{1,0:T(8,128)}, f32[512,256]{1,0:T(8,128)S(1)}, u32[]{:S(2)}) copy-start(f32[512,256]{1,0:T(8,128)S(1)} %get-tuple-element.89) | copy-start | bytes 1572868
  132.4 257.6 %reduce-scatter.13.cloned.1.call-start = ((), (), s32[]{:S(2)}) async-start(), calls=%async_computation.10 | async-start | bytes 1638400 | tf_op jit(solution)/shard_map/reduce_scatter | solution.py:151
  142.0 4.9 copy-start.59
  142.1 10.9 %copy-start.68 = (f32[256]{0:T(256)}, f32[256]{0:T(256)S(1)}, u32[]{:S(2)}) copy-start(f32[256]{0:T(256)S(1)} %get-tuple-element.100) | copy-start | bytes 3076
  142.1 25.3 %copy-start.70 = (f32[256]{0:T(256)}, f32[256]{0:T(256)S(1)}, u32[]{:S(2)}) copy-start(f32[256]{0:T(256)S(1)} %get-tuple-element.99) | copy-start | bytes 3076
  146.9 2.4 copy-start.64
  147.0 6.0 copy-start.5
  147.0 6.0 copy-start.56
  152.9 2.9 copy-start.51
  153.0 6.0 copy-start.23
  154.6 23.7 %copy-start.21 = (bf16[2,512,256]{2,1,0:T(8,128)(2,1)}, bf16[2,512,256]{2,1,0:T(8,128)(2,1)S(1)}, u32[]{:S(2)}) copy-start(bf16[2,512,256]{2,1,0:T(8,128)(2,1)S(1)} %fusion.65) | copy-start | bytes 1572868
  155.8 20.4 %collective-permute-start = (bf16[2,512,512]{2,1,0:T(8,128)(2,1)}, bf16[2,512,512]{2,1,0:T(8,128)(2,1)}, u32[]{:S(2)}, u32[]{:S(2)}) collective-permute-start(bf16[2,512,512]{2,1,0:T(8,128)(2,1)} %pad_maximum_fusion.2), channel_id=1, source_target_pairs={{0,1},{1,2},{2,3},{4,5},{5,6},{6,7},{8,9},{9,10},{10,11},{12,13},{... | collective-permute-start | bytes 3145736 | tf_op jit(solution)/shard_map/ppermute | solution.py:24
  160.1 2.2 copy-start.16
  160.4 5.1 copy-start.18
  165.5 2.2 copy-start.54
  169.5 8.8 %copy-start.37 = (bf16[2,512,4,256]{1,3,2,0:T(8,128)(2,1)}, bf16[2,512,4,256]{1,3,2,0:T(8,128)(2,1)S(1)}, u32[]{:S(2)}) copy-start(bf16[2,512,4,256]{1,3,2,0:T(8,128)(2,1)S(1)} %fusion.17) | copy-start | bytes 6291460
  178.3 10.2 %copy-start.34 = (bf16[2,512,256]{2,1,0:T(8,128)(2,1)}, bf16[2,512,256]{2,1,0:T(8,128)(2,1)S(1)}, u32[]{:S(2)}) copy-start(bf16[2,512,256]{2,1,0:T(8,128)(2,1)S(1)} %get-tuple-element.83) | copy-start | bytes 1572868
  202.1 2.8 copy-start.32
  220.4 7.3 copy-start.28
  227.7 3.6 copy-start.74
  227.7 3.7 copy-start.10
  234.5 12.8 %copy-start.42 = (bf16[1024,640]{1,0:T(8,128)(2,1)}, bf16[1024,640]{1,0:T(8,128)(2,1)S(1)}, u32[]{:S(2)}) copy-start(bf16[1024,640]{1,0:T(8,128)(2,1)S(1)} %get-tuple-element.75) | copy-start | bytes 3932164
  247.3 6.0 copy-start.75
  253.3 3.9 copy-start.9
  259.1 2.6 copy-start.45
  268.1 7.2 copy-start.52
  268.1 7.2 copy-start.53
  275.3 11.3 %copy-start.49 = (f32[2,1024,256]{2,1,0:T(8,128)}, f32[2,1024,256]{2,1,0:T(8,128)S(1)}, u32[]{:S(2)}) copy-start(f32[2,1024,256]{2,1,0:T(8,128)S(1)} %fusion.48) | copy-start | bytes 6291460
  286.7 11.7 %copy-start.38 = (bf16[2,512,4,256]{1,3,2,0:T(8,128)(2,1)S(1)}, bf16[2,512,4,256]{1,3,2,0:T(8,128)(2,1)}, u32[]{:S(2)}) copy-start(bf16[2,512,4,256]{1,3,2,0:T(8,128)(2,1)} %copy-done.37) | copy-start | bytes 6291460
  300.8 5.3 copy-start.24
  300.8 2.8 copy-start.20
  300.8 2.8 copy-start.22
  300.8 2.8 copy-start.35
  302.0 27.4 %collective-permute-start.2 = (bf16[2,512,512]{2,1,0:T(8,128)(2,1)}, bf16[2,512,512]{2,1,0:T(8,128)(2,1)}, u32[]{:S(2)}, u32[]{:S(2)}) collective-permute-start(bf16[2,512,512]{2,1,0:T(8,128)(2,1)} %pad_maximum_fusion.3), channel_id=1, source_target_pairs={{1,0},{2,1},{3,2},{5,4},{6,5},{7,6},{9,8},{10,9},{11,10},{13,12},{... | collective-permute-start | bytes 3145736 | tf_op jit(solution)/shard_map/ppermute | solution.py:24
  306.1 2.2 copy-start.1
  306.1 2.3 copy-start.39
  306.1 2.3 copy-start.55
  306.2 2.3 copy-start.71
  316.6 2.7 copy-start.33
  320.8 5.0 copy-start.19
  325.5 66.4 %reduce-scatter.9.cloned.1.call-start = ((), (), s32[]{:S(2)}) async-start(), calls=%async_computation.8 | async-start | bytes 3276800 | tf_op jit(solution)/shard_map/reduce_scatter | solution.py:151
  325.8 3.6 copy-start.14
  325.8 3.6 copy-start.25
  325.8 3.6 copy-start.50
  331.1 3.5 copy-start.29
  333.4 4.1 copy-start.36
  334.9 2.7 copy-start.73
  351.3 76.5 %reduce-scatter.21.cloned.1.call-start = ((), (), s32[]{:S(2)}) async-start(), calls=%async_computation.14 | async-start | bytes 3276800 | tf_op jit(solution)/shard_map/reduce_scatter | solution.py:151
  359.4 122.6 %reduce-scatter.17.cloned.1.call-start = ((), (), s32[]{:S(2)}) async-start(), calls=%async_computation.12 | async-start | bytes 6553600 | tf_op jit(solution)/shard_map/reduce_scatter | solution.py:151
  389.9 156.5 %reduce-scatter.15.cloned.1.call-start = ((), (), s32[]{:S(2)}) async-start(), calls=%async_computation.11 | async-start | bytes 368640 | tf_op jit(solution)/shard_map/reduce_scatter | solution.py:154
  391.8 219.1 %reduce-scatter.11.cloned.1.call-start = ((), (), s32[]{:S(2)}) async-start(), calls=%async_computation.9 | async-start | bytes 663552 | tf_op jit(solution)/shard_map/reduce_scatter | solution.py:154
  394.2 87.8 %copy-start.67 = (f32[1,4,2,128]{3,1,2,0:T(4,128)S(1)}, f32[1,4,2,128]{3,1,2,0:T(4,128)}, u32[]{:S(2)}) copy-start(f32[1,4,2,128]{3,1,2,0:T(4,128)} %copy-done.66) | copy-start | bytes 12292
  395.1 280.3 %reduce-scatter.23.cloned.1.call-start = ((), (), s32[]{:S(2)}) async-start(), calls=%async_computation.15 | async-start | bytes 737280 | tf_op jit(solution)/shard_map/reduce_scatter | solution.py:154
  429.9 312.3 %reduce-scatter.19.cloned.1.call-start = ((), (), s32[]{:S(2)}) async-start(), calls=%async_computation.13 | async-start | bytes 1474560 | tf_op jit(solution)/shard_map/reduce_scatter | solution.py:154
  (28 other events, 43.0 us)
Sparse Core Ops, SparseCore 0:
  42.4 19.1 all-gather.15
  64.3 45.7 all-gather.17
  111.6 23.3 all-gather.13
  136.5 25.5 all-gather.21
  163.5 40.4 all-gather.19
  325.6 27.5 reduce-scatter.12
  355.9 34.6 reduce-scatter.8
  393.1 34.7 reduce-scatter.20
  430.6 51.3 reduce-scatter.16
  485.1 61.3 reduce-scatter.14
  549.7 61.1 reduce-scatter.10
  614.4 61.0 reduce-scatter.22
  678.8 63.3 reduce-scatter.18
